TPU v7x, 256 devices: a whole 4x4x8 slice. The times are simulated.
256 devices in a mesh: ctx: 16 (over y_lo, x, core), fsdp: 16 (over z, y_hi).
Axes of the slice: x: 4, y: 4 (y_hi: 2, y_lo: 2; y = y_hi * 2 + y_lo), z: 8, core: 2. Of those that a mesh axis runs over, the one named last changes fastest.
Arguments:
- x_t: bfloat16 [32, 1024, 1536], P('fsdp', 'ctx'), may hold values from -6 to 6
- clip_len: int32 [32], P('fsdp'), may hold values from 1 to 1024, as said below
- time_idx: int32 [32], P('fsdp'), may hold values from 0 to 999
- teacher_mod: float32 [2, 1536], replicated, may hold values from -2 to 2
- student_mod: float32 [2, 1536], replicated, may hold values from -2 to 2
- w_qkv: bfloat16 [1536, 6144], P('fsdp'), may hold values from -1 to 1
- w_out: bfloat16 [2048, 1536], P('fsdp'), may hold values from -0.125 to 0.125
Outputs:
- student_out: bfloat16 [32, 1024, 1536], P('fsdp', 'ctx')
- student_tangent: bfloat16 [32, 1024, 1536], P('fsdp', 'ctx')
Inputs may be any that keep to these rules, and one draw needn't show every extreme that they name: `clip_len`: every draw has a clip of exactly 1024 live tokens and a short clip of at most 128.
All inputs are finite; a program needn't handle non-finite values.
Results may differ from a plain program's by a relative error of at most 0.015.
The roundings to bfloat16 on the way count: a program that leaves them out, or rounds other values in their place, can miss the bound.
Values may be sent and summed in bfloat16 or wider, within the bound.
A program may use at most 128 MiB of HBM per device.

v0:
```python
import math

import jax
import jax.numpy as jnp
from jax import lax
from jax.sharding import PartitionSpec as P

HEADS = 16
HD = 128
TIME_STEPS = 1000


def softmax_parts(query, keys, live):
    scale = 1.0 / math.sqrt(HD)
    scores = jnp.einsum("qhd,khd->hqk", query, keys, preferred_element_type=jnp.float32) * scale
    scores = jnp.where(live[None, None, :], scores, -1e30)
    top = jnp.max(scores, axis=-1, keepdims=True)
    expo = jnp.exp(scores - top)
    probs = expo / jnp.sum(expo, axis=-1, keepdims=True)
    return (probs, probs.astype(jnp.bfloat16))


def teacher_clip(args):
    packed, live = args
    probs, weights = softmax_parts(packed[:, 0], packed[:, 1], live)
    out = jnp.einsum("hqk,khd->qhd", weights, packed[:, 2], preferred_element_type=jnp.float32)
    return out.astype(jnp.bfloat16)


def student_clip(args):
    packed, tangent, live = args
    scale = 1.0 / math.sqrt(HD)
    query, keys, values = (packed[:, 0], packed[:, 1], packed[:, 2])
    dquery, dkeys, dvalues = (tangent[:, 0], tangent[:, 1], tangent[:, 2])
    probs, weights = softmax_parts(query, keys, live)
    out = jnp.einsum("hqk,khd->qhd", weights, values, preferred_element_type=jnp.float32)
    dscore = jnp.einsum("qhd,khd->hqk", dquery, keys, preferred_element_type=jnp.float32)
    dscore = (
        dscore + jnp.einsum("qhd,khd->hqk", query, dkeys, preferred_element_type=jnp.float32)
    ) * scale
    dprob = probs * (dscore - jnp.sum(probs * dscore, axis=-1, keepdims=True))
    dout = jnp.einsum(
        "hqk,khd->qhd", dprob.astype(jnp.bfloat16), values, preferred_element_type=jnp.float32
    )
    dout = dout + jnp.einsum("hqk,khd->qhd", weights, dvalues, preferred_element_type=jnp.float32)
    return (out.astype(jnp.bfloat16), dout.astype(jnp.bfloat16))


def on_device(x_t, clip_len, time_idx, teacher_mod, student_mod, w_qkv, w_out):
    clips, seg, width = x_t.shape
    rows = clips * seg
    inner = HEADS * HD
    angle = math.pi / 2 * (time_idx.astype(jnp.float32) + 0.5) / TIME_STEPS
    sin_t = jnp.sin(angle)[:, None, None]
    cos_t = jnp.cos(angle)[:, None, None]
    latent_f = x_t.astype(jnp.float32)
    rstd = lax.rsqrt(jnp.mean(latent_f * latent_f, axis=-1, keepdims=True) + 1e-06)
    normed = latent_f * rstd
    gain_teacher = 1.0 + sin_t * teacher_mod[0] + cos_t * teacher_mod[1]
    h_teacher = (normed * gain_teacher).astype(jnp.bfloat16).reshape(rows, width)
    qkv_full, out_full = (
        lax.all_gather(w_qkv, "fsdp", axis=0, tiled=True),
        lax.all_gather(w_out, "fsdp", axis=0, tiled=True),
    )
    qkv_teacher = jnp.dot(h_teacher, qkv_full, preferred_element_type=jnp.float32)
    packed_teacher = qkv_teacher.astype(jnp.bfloat16).reshape(clips, seg, 3, HEADS, HD)
    spread_teacher = lax.all_to_all(packed_teacher, "ctx", split_axis=3, concat_axis=1, tiled=True)
    teacher_live = jnp.arange(spread_teacher.shape[1], dtype=jnp.int32)[None, :] < clip_len[:, None]
    mixed_teacher = lax.map(teacher_clip, (spread_teacher, teacher_live))
    attn_teacher = lax.all_to_all(mixed_teacher, "ctx", split_axis=1, concat_axis=2, tiled=True)
    velocity = jnp.dot(
        attn_teacher.reshape(rows, inner), out_full, preferred_element_type=jnp.float32
    ).astype(jnp.bfloat16)
    gain_student = 1.0 + sin_t * student_mod[0] + cos_t * student_mod[1]
    dgain_student = cos_t * student_mod[0] - sin_t * student_mod[1]
    h_student = (normed * gain_student).astype(jnp.bfloat16).reshape(rows, width)
    vel_f = velocity.astype(jnp.float32).reshape(clips, seg, width)
    cross = jnp.mean(latent_f * vel_f, axis=-1, keepdims=True)
    dnormed = rstd * vel_f - latent_f * rstd * rstd * rstd * cross
    dh_student = (
        (dnormed * gain_student + normed * dgain_student).astype(jnp.bfloat16).reshape(rows, width)
    )
    stacked = jnp.concatenate([h_student, dh_student], axis=0)
    qkv_both = jnp.dot(stacked, qkv_full, preferred_element_type=jnp.float32).astype(jnp.bfloat16)
    packed_student = qkv_both[:rows].reshape(clips, seg, 3, HEADS, HD)
    packed_tangent = qkv_both[rows:].reshape(clips, seg, 3, HEADS, HD)
    spread_student, spread_tangent = (
        lax.all_to_all(packed_student, "ctx", split_axis=3, concat_axis=1, tiled=True),
        lax.all_to_all(packed_tangent, "ctx", split_axis=3, concat_axis=1, tiled=True),
    )
    student_live = jnp.arange(spread_student.shape[1], dtype=jnp.int32)[None, :] < clip_len[:, None]
    mixed_student, mixed_tangent = lax.map(
        student_clip, (spread_student, spread_tangent, student_live)
    )
    attn_student, dattn_student = (
        lax.all_to_all(mixed_student, "ctx", split_axis=1, concat_axis=2, tiled=True),
        lax.all_to_all(mixed_tangent, "ctx", split_axis=1, concat_axis=2, tiled=True),
    )
    joined = jnp.concatenate(
        [attn_student.reshape(rows, inner), dattn_student.reshape(rows, inner)], axis=0
    )
    projected = jnp.dot(joined, out_full, preferred_element_type=jnp.float32).astype(jnp.bfloat16)
    student_out = projected[:rows].reshape(clips, seg, width)
    student_tangent = projected[rows:].reshape(clips, seg, width)
    return (student_out, student_tangent)


def solution(mesh):
    in_specs = (
        P("fsdp", "ctx", None),
        P("fsdp"),
        P("fsdp"),
        P(),
        P(),
        P("fsdp", None),
        P("fsdp", None),
    )
    out_specs = (P("fsdp", "ctx", None), P("fsdp", "ctx", None))
    return jax.shard_map(
        on_device, mesh=mesh, in_specs=in_specs, out_specs=out_specs, check_vma=False
    )
```

profile of v0, /device:TPU:1, one launch (start us, length us, event | category | flops | bytes accessed | tf_op | source)
XLA Modules:
  0.0 532.6 jit_solution(10040069925647208363)
XLA Ops:
  8.6 0.9 slice_reduce_fusion.1
  9.5 1.2 fusion.44
  11.5 1.2 fusion.41
  12.6 249.9 %all-gather.3.cloned.1.call-done = bf16[1536,6144]{1,0:T(8,128)(2,1)} async-done(((bf16[96,6144]{1,0:T(8,128)(2,1)}), bf16[1536,6144]{1,0:T(8,128)(2,1)}) %all-gather.3.cloned.1.call-update) | async-done | bytes 18874384 | tf_op jit(solution)/shard_map/all_gather | solution.py:62
  262.6 9.0 %fusion.28 = bf16[16,8,48,128]{3,1,2,0:T(8,128)(2,1)S(1)} fusion(bf16[128,1536]{1,0:T(8,128)(2,1)S(1)} %bitcast.192, bf16[1536,6144]{1,0:T(8,128)(2,1)} %all-gather.3.cloned.1.call-done), kind=kOutput, calls=%fused_computation.54 | convolution fusion | flops 2416705536 | bytes 20840448 | tf_op jit(solution)/shard_map/dot_general | solution.py:65
  272.0 1.7 copy.24
  273.6 5.4 %all-to-all-start = ((bf16[2,64,3,16,128]{4,1,2,0,3:T(8,128)(2,1)}), bf16[2,64,3,16,128]{4,1,2,0,3:T(8,128)(2,1)S(1)}, u32[]{:S(2)}, u32[]{:S(2)}) async-start(bf16[2,64,3,16,128]{4,1,2,0,3:T(8,128)(2,1)} %copy.24), calls=%async_computation | async-start | bytes 3145728 | tf_op jit(solution)/shard_map/all_to_all | solution.py:67
  279.1 21.4 %all-to-all-done = bf16[2,64,3,16,128]{4,1,2,0,3:T(8,128)(2,1)S(1)} async-done(((bf16[2,64,3,16,128]{4,1,2,0,3:T(8,128)(2,1)}), bf16[2,64,3,16,128]{4,1,2,0,3:T(8,128)(2,1)S(1)}, u32[]{:S(2)}, u32[]{:S(2)}) %all-to-all-start) | async-done | bytes 1572896 | tf_op jit(solution)/shard_map/all_to_all | solution.py:67
  300.8 6.4 %while.22 = (s32[]{:T(128)}, bf16[2,1024,1,128]{1,3,2,0:T(8,128)(2,1)S(1)}, bf16[2,1024,3,1,128]{4,1,3,2,0:T(8,128)(2,1)S(1)}, pred[2,1024]{1,0:T(4,128)(4,1)S(1)}, s32[]{:T(128)}) while((s32[]{:T(128)}, bf16[2,1024,1,128]{1,3,2,0:T(8,128)(2,1)S(1)}, bf16[2,1024,3,1,128]{4,1,3,2,0:T(8,128)(2,1)S(1)}, pred[2,1024]{1,0:T(4,128)(4,1)S(1)}, ...), condition=%wide.region_4.5_spmd, body=%wide.region_1.4_spmd.sunk | while | flops 549582848 | bytes 15230025 | solution.py:69
  300.9 0.7 fusion.72
  301.6 0.9 fusion.73
  302.5 1.4 fusion.74
  304.8 0.9 fusion.73
  305.7 1.4 fusion.74
  307.5 13.7 %all_to_all.99 = bf16[2,1024,1,128]{3,0,2,1:T(2,128)(2,1)S(1)} all-to-all(bf16[2,1024,1,128]{3,0,2,1:T(2,128)(2,1)S(1)} %copy.27), channel_id=1, replica_groups=mesh['ctx'=16,'fsdp'=16] {'ctx'}, dimensions={1} | all-to-all | bytes 1048576 | tf_op jit(solution)/shard_map/all_to_all | solution.py:70
  321.7 71.5 %all-gather.5.cloned.1.call-done = bf16[2048,1536]{1,0:T(8,128)(2,1)} async-done(((bf16[128,1536]{1,0:T(8,128)(2,1)}), bf16[2048,1536]{1,0:T(8,128)(2,1)}) %all-gather.5.cloned.1.call-update) | async-done | bytes 6291472 | tf_op jit(solution)/shard_map/all_gather | solution.py:63
  393.2 3.8 convolution_convert_fusion.4
  397.6 11.8 %convolution_convert_fusion.1 = bf16[256,6144]{1,0:T(8,128)(2,1)S(1)} fusion(bf16[1536,6144]{1,0:T(8,128)(2,1)} %all-gather.3.cloned.1.call-done, bf16[128,1536]{1,0:T(8,128)(2,1)S(1)} %bitcast.198, bf16[128,1536]{1,0:T(8,128)(2,1)S(1)} %bitcast.197), kind=kOutput, calls=%fused_computation.48 | convolution fusion | flops 4834983936 | bytes 22806528 | tf_op jit(solution)/shard_map/dot_general | solution.py:84
  410.1 1.6 copy.30
  411.7 5.9 %all-to-all-start.2 = ((bf16[2,64,3,16,128]{4,1,2,0,3:T(8,128)(2,1)}), bf16[2,64,3,16,128]{4,1,2,0,3:T(8,128)(2,1)S(1)}, u32[]{:S(2)}, u32[]{:S(2)}) async-start(bf16[2,64,3,16,128]{4,1,2,0,3:T(8,128)(2,1)} %copy.30), calls=%async_computation.2 | async-start | bytes 3145728 | tf_op jit(solution)/shard_map/all_to_all | solution.py:88
  418.0 1.6 copy.32
  419.5 19.5 %all-to-all-done.2 = bf16[2,64,3,16,128]{4,1,2,0,3:T(8,128)(2,1)S(1)} async-done(((bf16[2,64,3,16,128]{4,1,2,0,3:T(8,128)(2,1)}), bf16[2,64,3,16,128]{4,1,2,0,3:T(8,128)(2,1)S(1)}, u32[]{:S(2)}, u32[]{:S(2)}) %all-to-all-start.2) | async-done | bytes 1572896 | tf_op jit(solution)/shard_map/all_to_all | solution.py:88
  439.1 4.8 all-to-all-start.3
  444.1 21.5 %all-to-all-done.3 = bf16[2,64,3,16,128]{4,1,2,0,3:T(8,128)(2,1)} async-done(((bf16[2,64,3,16,128]{4,1,2,0,3:T(8,128)(2,1)}), bf16[2,64,3,16,128]{4,1,2,0,3:T(8,128)(2,1)}, u32[]{:S(2)}, u32[]{:S(2)}) %all-to-all-start.3) | async-done | bytes 1572896 | tf_op jit(solution)/shard_map/all_to_all | solution.py:89
  465.6 1.6 copy.33
  467.1 0.9 broadcast.176
  468.0 0.9 broadcast.176.clone
  468.9 20.3 %while.23 = (s32[]{:T(128)}, bf16[2,1024,1,128]{1,3,2,0:T(8,128)(2,1)}, bf16[2,1024,1,128]{1,3,2,0:T(8,128)(2,1)}, bf16[2,1024,3,1,128]{4,1,3,2,0:T(8,128)(2,1)S...) while((s32[]{:T(128)}, ...), condition=%wide.region_10.11_spmd, body=%wide.region_6.10_spmd.sunk | while | flops 1644557312 | bytes 49083476 | solution.py:92
  469.0 0.7 fusion.77
  469.8 0.9 fusion.78
  471.4 1.8 multiply_reduce_fusion.2
  473.2 1.4 fusion.80
  474.6 2.4 fusion.82
  476.9 2.1 fusion.79
  479.2 0.7 fusion.77
  479.9 0.9 fusion.78
  481.5 1.8 multiply_reduce_fusion.2
  483.3 1.4 fusion.80
  484.7 2.4 fusion.82
  487.1 2.1 fusion.79
  489.2 2.0 copy.39
  491.2 4.1 all-to-all-start.5
  495.3 2.0 copy.36
  497.3 8.0 %all-to-all-done.5 = bf16[2,1024,1,128]{3,0,2,1:T(2,128)(2,1)S(1)} async-done(((bf16[2,1024,1,128]{3,0,2,1:T(2,128)(2,1)}), bf16[2,1024,1,128]{3,0,2,1:T(2,128)(2,1)S(1)}, u32[]{:S(2)}, u32[]{:S(2)}) %all-to-all-start.5) | async-done | bytes 524320 | tf_op jit(solution)/shard_map/all_to_all | solution.py:97
  505.3 4.4 all-to-all-start.4
  510.2 9.4 %all-to-all-done.4 = bf16[2,1024,1,128]{3,0,2,1:T(2,128)(2,1)S(1)} async-done(((bf16[2,1024,1,128]{3,0,2,1:T(2,128)(2,1)}), bf16[2,1024,1,128]{3,0,2,1:T(2,128)(2,1)S(1)}, u32[]{:S(2)}, u32[]{:S(2)}) %all-to-all-start.4) | async-done | bytes 524320 | tf_op jit(solution)/shard_map/all_to_all | solution.py:96
  520.2 4.6 convolution_convert_fusion.3
  524.8 0.9 fusion.55
  (42 shorter events, 9.2 us)
Async XLA Ops:
  7.2 255.4 %all-gather.3.cloned.1.call-start = ((), (), s32[]{:S(2)}) async-start(), calls=%async_computation.6 | async-start | bytes 20054016 | tf_op jit(solution)/shard_map/all_gather | solution.py:62
  7.9 385.3 %all-gather.5.cloned.1.call-start = ((), (), s32[]{:S(2)}) async-start(), calls=%async_computation.7 | async-start | bytes 6684672 | tf_op jit(solution)/shard_map/all_gather | solution.py:63
  271.6 7.5 %copy-start.1 = (s32[2]{0:T(128)S(1)}, s32[2]{0:T(128)}, u32[]{:S(2)}) copy-start(s32[2]{0:T(128)} %param.12) | copy-start | bytes 28
  273.6 26.9 %all-to-all-start = ((bf16[2,64,3,16,128]{4,1,2,0,3:T(8,128)(2,1)}), bf16[2,64,3,16,128]{4,1,2,0,3:T(8,128)(2,1)S(1)}, u32[]{:S(2)}, u32[]{:S(2)}) async-start(bf16[2,64,3,16,128]{4,1,2,0,3:T(8,128)(2,1)} %copy.24), calls=%async_computation | async-start | bytes 3145728 | tf_op jit(solution)/shard_map/all_to_all | solution.py:67
  321.3 75.7 %copy-start = (bf16[2,64,1536]{2,1,0:T(8,128)(2,1)S(1)}, bf16[2,64,1536]{2,1,0:T(8,128)(2,1)}, u32[]{:S(2)}) copy-start(bf16[2,64,1536]{2,1,0:T(8,128)(2,1)} %param.11) | copy-start | bytes 1179652
  411.7 27.3 %all-to-all-start.2 = ((bf16[2,64,3,16,128]{4,1,2,0,3:T(8,128)(2,1)}), bf16[2,64,3,16,128]{4,1,2,0,3:T(8,128)(2,1)S(1)}, u32[]{:S(2)}, u32[]{:S(2)}) async-start(bf16[2,64,3,16,128]{4,1,2,0,3:T(8,128)(2,1)} %copy.30), calls=%async_computation.2 | async-start | bytes 3145728 | tf_op jit(solution)/shard_map/all_to_all | solution.py:88
  439.1 26.5 %all-to-all-start.3 = ((bf16[2,64,3,16,128]{4,1,2,0,3:T(8,128)(2,1)}), bf16[2,64,3,16,128]{4,1,2,0,3:T(8,128)(2,1)}, u32[]{:S(2)}, u32[]{:S(2)}) async-start(bf16[2,64,3,16,128]{4,1,2,0,3:T(8,128)(2,1)} %copy.32), calls=%async_computation.3 | async-start | bytes 3145728 | tf_op jit(solution)/shard_map/all_to_all | solution.py:89
  491.2 14.1 %all-to-all-start.5 = ((bf16[2,1024,1,128]{3,0,2,1:T(2,128)(2,1)}), bf16[2,1024,1,128]{3,0,2,1:T(2,128)(2,1)S(1)}, u32[]{:S(2)}, u32[]{:S(2)}) async-start(bf16[2,1024,1,128]{3,0,2,1:T(2,128)(2,1)} %copy.39), calls=%async_computation.5 | async-start | bytes 1048576 | tf_op jit(solution)/shard_map/all_to_all | solution.py:97
  505.3 14.4 %all-to-all-start.4 = ((bf16[2,1024,1,128]{3,0,2,1:T(2,128)(2,1)}), bf16[2,1024,1,128]{3,0,2,1:T(2,128)(2,1)S(1)}, u32[]{:S(2)}, u32[]{:S(2)}) async-start(bf16[2,1024,1,128]{3,0,2,1:T(2,128)(2,1)} %copy.36), calls=%async_computation.4 | async-start | bytes 1048576 | tf_op jit(solution)/shard_map/all_to_all | solution.py:96
Sparse Core Ops, SparseCore 0:
  10.6 251.9 all-gather.2
  265.2 128.0 all-gather.4
where the time goes:
time: 533 us
  waiting for transfers between devices  403 us (76%)
  matrix products  51.6 us (10%)
  starting transfers between devices  24.7 us (5%)
  local copies, waits for them, and re-layouts  18 us (3%)
  between operations  14.3 us (3%)
  blocking collectives  13.7 us (3%)
  other arithmetic  7.49 us (1%)
    all_gather x1, waiting for transfers between devices, on_device(): lax.all_gather(w_qkv, 'fsdp', axis=0, tiled=True)  250 us
    all_gather x1, waiting for transfers between devices, on_device(): lax.all_gather(w_out, 'fsdp', axis=0, tiled=True)  71.5 us
    all_to_all x1, waiting for transfers between devices, on_device(): lax.all_to_all(packed_tangent, 'ctx', split_axis=3, concat_axis=1, tiled=...  21.5 us
    all_to_all x1, waiting for transfers between devices, on_device(): lax.all_to_all(packed_teacher, 'ctx', split_axis=3, concat_axis=1, tiled=...  21.4 us
    all_to_all x1, waiting for transfers between devices, on_device(): lax.all_to_all(packed_student, 'ctx', split_axis=3, concat_axis=1, tiled=...  19.5 us
    all_to_all x1, blocking collectives, on_device(): lax.all_to_all(mixed_teacher, 'ctx', split_axis=1, concat_axis=2, tiled=T...  13.7 us
    dot_general x1, matrix products, on_device(): jnp.dot(stacked, qkv_full, preferred_element_type=jnp.float32)  11.8 us
  transfers between devices with their start and end apart: 7, of which 7 were waited for; matrix products, arithmetic and copies ran while one was open for 5% of the time, Pallas kernels for 0%

commit v1 on v0

v1 whole, which is shorter than its diff:
```python
import functools
import math

import jax
import jax.numpy as jnp
from jax import lax
from jax.experimental import pallas as pl
from jax.experimental.pallas import tpu as pltpu
from jax.sharding import PartitionSpec as P

HEADS = 16
HD = 128
TIME_STEPS = 1000
D = 1536
INNER = HEADS * HD
SEG = 64
CLIPS = 2
SLOTS = 8
HALF = SLOTS * SEG
FULL = 2 * HALF
BLK = 4 * SEG
SCALE = 1.0 / math.sqrt(HD)
EXP2_SCALE = SCALE * math.log2(math.e)
MESH = pl.DeviceIdType.MESH
F32 = jnp.float32
BF16 = jnp.bfloat16

S00, S01, S03, S10, S02, S11, S13, S12 = range(8)


def mult(value, by):
    return pl.multiple_of(value, by)


def kernel(
    len_ref, time_ref, x_ref, tmod_ref, smod_ref, wqkv_ref, wout_ref,
    student_ref, tangent_ref,
    xg, dg, wq, wo, qkv_t, qkv_s, qkv_d, other_t, other_s, other_d, hbuf, gains, kmask,
    mixed_t, mixed_s, mixed_d, attn_t, attn_s, attn_d, vel, dh, scaled, weights,
    send, recv, local, bulk_send, bulk_recv,
):
    c = lax.axis_index("ctx")
    f = lax.axis_index("fsdp")
    core = c % 2
    chip = c // 2
    xx = chip % 4
    yl = c // 8
    z = f // 2
    yh = f % 2

    def device(dcore=0, dx=0, dyl=0, dz=0, dyh=0):
        ctx = ((yl + dyl) % 2 * 4 + (xx + dx) % 4) * 2 + (core + dcore) % 2
        return (ctx, (z + dz) % 8 * 2 + (yh + dyh) % 2)

    sibling = device(dcore=1)
    x_up, x_down = device(dx=1), device(dx=3)
    y_in = device(dyl=1)
    y_out = device(dyl=1, dyh=1)
    z_up, z_down = device(dz=1), device(dz=7)

    barrier = pltpu.get_barrier_semaphore()
    partners = [y_out, z_up, z_down]
    for dyl in range(2):
        for dx in range(4):
            for dcore in range(2):
                if dyl + dx + dcore:
                    partners.append(device(dcore=dcore, dx=dx, dyl=dyl))
    for partner in partners:
        pl.semaphore_signal(barrier, inc=1, device_id=partner, device_id_type=MESH)

    used = [0]
    started = []

    def remote(src, dst, where):
        number = used[0]
        used[0] += 1
        copy = pltpu.make_async_remote_copy(
            src_ref=src, dst_ref=dst, send_sem=send.at[number], recv_sem=recv.at[number],
            device_id=where, device_id_type=MESH,
        )
        copy.start()
        started.append(copy)
        return copy

    nlocal = [0]

    def here(src, dst):
        copy = pltpu.make_async_copy(src, dst, local.at[nlocal[0]])
        nlocal[0] += 1
        copy.start()
        return copy

    def arrived(*copies):
        for copy in copies:
            copy.wait_recv()

    class Gather:
        def __init__(self, own, buf):
            self.own, self.buf = own, buf

        def slot(self, clip, slot, lo=0, n=SEG):
            return self.buf.at[pl.ds(clip * HALF + slot * SEG + lo, n)]

        def mine(self, clip):
            return self.own.at[pl.ds(clip * SEG, SEG)]

        def begin(self):
            self.b_up = remote(self.mine(1), self.slot(1, S03), x_up)
            self.b_down = remote(self.mine(1), self.slot(1, S01), x_down)
            self.a_y = remote(self.mine(0), self.slot(0, S10), y_in)
            self.a_up = remote(self.mine(0), self.slot(0, S03), x_up)
            self.a_down = remote(self.mine(0), self.slot(0, S01), x_down)
            self.b_y = remote(self.mine(1), self.slot(1, S10), y_in)
            self.self0 = here(self.mine(0), self.slot(0, S00))
            self.self1 = here(self.mine(1), self.slot(1, S00))

        def step1(self):
            arrived(self.b_up)
            self.b_h_up = remote(self.slot(1, S03, 0, 32), self.slot(1, S02, 0, 32), x_up)
            arrived(self.b_down)
            self.b_h_down = remote(self.slot(1, S01, 32, 32), self.slot(1, S02, 32, 32), x_down)
            self.b_y1 = remote(self.slot(1, S01), self.slot(1, S11), y_in)
            self.b_y3 = remote(self.slot(1, S03), self.slot(1, S13), y_in)

        def step2(self):
            arrived(self.a_y)
            self.a_y_up = remote(self.slot(0, S10), self.slot(0, S13), x_up)
            self.a_y_down = remote(self.slot(0, S10), self.slot(0, S11), x_down)

        def step3(self):
            arrived(self.a_up)
            self.a_h_up = remote(self.slot(0, S03, 0, 32), self.slot(0, S02, 0, 32), x_up)
            arrived(self.a_down)
            self.a_h_down = remote(self.slot(0, S01, 32, 32), self.slot(0, S02, 32, 32), x_down)

        def step4(self):
            arrived(self.b_h_up, self.b_h_down)
            self.b_y2 = remote(self.slot(1, S02), self.slot(1, S12), y_in)
            arrived(self.b_y)
            self.self0.wait()
            self.self1.wait()

        def step5(self):
            arrived(self.a_y_up)
            self.a_yh_up = remote(self.slot(0, S13, 0, 32), self.slot(0, S12, 0, 32), x_up)
            arrived(self.a_y_down)
            self.a_yh_down = remote(self.slot(0, S11, 32, 32), self.slot(0, S12, 32, 32), x_down)

        def end_a(self):
            arrived(self.a_h_up, self.a_h_down, self.a_yh_up, self.a_yh_down)

        def end_b(self):
            arrived(self.b_y1, self.b_y3, self.b_y2)

    class Ring:
        def __init__(self, buf, rows, cols, core_cols):
            self.buf, self.rows, self.cols, self.core_cols = buf, rows, cols, core_cols
            self.cores = []

        def block(self, dz, part=None):
            base = mult((z + dz) % 8 * (2 * self.rows), 16)
            if part is None:
                return self.buf.at[pl.ds(base, 2 * self.rows), self.cols]
            return self.buf.at[pl.ds(base + part * self.rows, self.rows), self.cols]

        def share(self, dz):
            base = mult((z + dz) % 8 * (2 * self.rows), 16)
            self.cores.append(remote(
                self.block(dz), self.buf.at[pl.ds(base, 2 * self.rows), self.core_cols], sibling))

        def step1(self):
            self.up = remote(self.block(0), self.block(0), z_up)
            self.down = remote(self.block(0), self.block(0), z_down)
            self.share(0)

        def step(self, k):
            arrived(self.up)
            if k < 4:
                self.up = remote(self.block(-k + 1), self.block(-k + 1), z_up)
            arrived(self.down)
            if k < 4:
                self.down = remote(self.block(k - 1), self.block(k - 1), z_down)
            self.share(8 - k + 1)
            self.share(k - 1)

        def step4(self):
            arrived(self.up)
            self.up = remote(self.block(-3, 0), self.block(-3, 0), z_up)
            arrived(self.down)
            self.down = remote(self.block(3, 1), self.block(3, 1), z_down)
            self.share(5)
            self.share(3)

        def last(self):
            arrived(self.up, self.down)
            self.share(4)

        def end(self):
            arrived(*self.cores)

    pl.semaphore_wait(barrier, len(partners))

    gx = Gather(x_ref, xg)
    gx.begin()
    c_out = (c + 8) % 16
    row_q = mult(f * 96, 16)
    hop_q = [
        remote(
            wqkv_ref.at[:, pl.ds(mult(part * INNER + c_out * HD, HD), HD)],
            wq.at[pl.ds(row_q, 96), pl.ds(part * HD, HD)], y_out)
        for part in range(3)
    ]
    own_q = [
        here(
            wqkv_ref.at[:, pl.ds(mult(part * INNER + c * HD, HD), HD)],
            wq.at[pl.ds(row_q, 96), pl.ds(part * HD, HD)])
        for part in range(3)
    ]
    my_cols = pl.ds(mult(core * 768, HD), 768)
    row_o = mult(f * HD, HD)
    hop_o = remote(wout_ref.at[:, my_cols], wo.at[pl.ds(row_o, HD), my_cols], y_out)
    own_o = here(wout_ref.at[:, my_cols], wo.at[pl.ds(row_o, HD), my_cols])
    rq = Ring(wq, 96, pl.ds(0, 384), pl.ds(384, 384))
    ro = Ring(wo, HD, my_cols, my_cols)

    for clip in range(CLIPS):
        angle = jnp.full((1, D), time_ref[clip].astype(F32), F32)
        angle = math.pi / 2 * (angle + 0.5) / TIME_STEPS
        sin_t, cos_t = jnp.sin(angle), jnp.cos(angle)
        gains[pl.ds(clip * 3, 1)] = 1.0 + sin_t * tmod_ref[0:1] + cos_t * tmod_ref[1:2]
        gains[pl.ds(clip * 3 + 1, 1)] = 1.0 + sin_t * smod_ref[0:1] + cos_t * smod_ref[1:2]
        gains[pl.ds(clip * 3 + 2, 1)] = cos_t * smod_ref[0:1] - sin_t * smod_ref[1:2]
    within = lax.broadcasted_iota(jnp.int32, (SEG, HD), 0)
    lane0 = lax.broadcasted_iota(jnp.int32, (SEG, HD), 1) == 0
    places = ((0, 0), (0, 1), (0, 3), (1, 0), (0, 2), (1, 1), (1, 3), (1, 2))
    for clip in range(CLIPS):
        for half in range(2):
            for slot, (dyl, dx) in enumerate(places):
                token = within + device(dcore=half, dx=dx, dyl=dyl)[0] * SEG
                dead = jnp.logical_and(token >= len_ref[clip], lane0)
                kmask[pl.ds(clip * FULL + half * HALF + slot * SEG, SEG)] = jnp.where(
                    dead, -1e30, 0.0).astype(BF16)
    one0 = jnp.where(lax.broadcasted_iota(jnp.int32, (BLK, HD), 1) == 0, 1.0, 0.0).astype(BF16)

    def project(source, base, out, other):
        y = jnp.dot(source, wq[...], preferred_element_type=F32).astype(BF16)
        clip, rest = base // HALF, base % HALF
        out[pl.ds(mult(clip * FULL + rest, BLK), BLK)] = y[:, :384]
        other[pl.ds(mult(base, BLK), BLK)] = y[:, 384:]

    def chunk(base, gain_row, out, other):
        def piece(i, _):
            xf = xg[pl.ds(mult(base + i * 32, 32), 32)].astype(F32)
            rstd = lax.rsqrt(jnp.mean(xf * xf, axis=-1, keepdims=True) + 1e-6)
            hbuf[pl.ds(mult(i * 32, 32), 32)] = (xf * rstd * gains[pl.ds(gain_row, 1)]).astype(BF16)
            return 0

        lax.fori_loop(0, BLK // 32, piece, 0)
        project(hbuf[...], base, out, other)

    def exchange(clip, group, out, other):
        return remote(
            other.at[pl.ds(clip * HALF + group * BLK, BLK)],
            out.at[pl.ds(clip * FULL + HALF + group * BLK, BLK)], sibling)

    def send_block(blk, phase, mixed, attn):
        clip = blk // 4
        half = blk // 2 % 2
        group = blk % 2
        steps = ((0, 2 * group), (group, 1), (group, 3), (1, 2 * group))
        for j, (dyl, dx) in enumerate(steps):
            where = device(dcore=half, dx=dx, dyl=dyl)
            src = mixed.at[pl.ds(mult(blk * BLK + j * SEG, SEG), SEG)]
            dst = attn.at[pl.ds(mult(clip * SEG, SEG), SEG), pl.ds(mult(c * HD, HD), HD)]

            def away(src=src, dst=dst, where=where):
                pltpu.make_async_remote_copy(
                    src_ref=src, dst_ref=dst, send_sem=bulk_send.at[phase],
                    recv_sem=bulk_recv.at[phase], device_id=where, device_id_type=MESH,
                ).start()

            if j == 0:
                stays = half + group == 0

                @pl.when(stays)
                def _(src=src, dst=dst):
                    pltpu.make_async_copy(src, dst, bulk_recv.at[phase]).start()

                pl.when(jnp.logical_not(stays))(away)
            else:
                away()

    def all_received(phase, attn):
        pltpu.make_async_copy(attn, attn, bulk_recv.at[phase]).wait()

    def all_sent(phase, attn):
        part = attn.at[:, pl.ds(0, INNER - HD)]
        pltpu.make_async_copy(part, part, bulk_send.at[phase]).wait()

    NT = (((1,), (1,)), ((), ()))

    def scores_of(blk, qkv):
        clip = blk // 4
        rows = pl.ds(mult(blk * BLK, BLK), BLK)
        keys = pl.ds(mult(clip * FULL, FULL), FULL)
        query = jnp.concatenate([qkv[rows, 0:HD], one0], axis=1)
        key = jnp.concatenate([qkv[keys, HD:2 * HD], kmask[keys]], axis=1)
        scores = lax.dot_general(query, key, NT, preferred_element_type=F32)
        top = jnp.max(scores, axis=-1, keepdims=True)
        expo = jnp.exp2((scores - top) * EXP2_SCALE)
        return rows, keys, expo, jnp.sum(expo, axis=-1, keepdims=True)

    def teacher_block(blk, _):
        rows, keys, expo, total = scores_of(blk, qkv_t)
        out = jnp.dot(expo.astype(BF16), qkv_t[keys, 2 * HD:], preferred_element_type=F32)
        mixed_t[rows] = (out / total).astype(BF16)
        send_block(blk, 0, mixed_t, attn_t)
        return 0

    def student_block(blk, _):
        rows, keys, expo, total = scores_of(blk, qkv_s)
        probs = expo * (1.0 / total)
        weight = probs.astype(BF16)
        weights[rows] = weight
        scaled[rows] = probs * SCALE
        mixed_s[rows] = jnp.dot(
            weight, qkv_s[keys, 2 * HD:], preferred_element_type=F32).astype(BF16)
        return 0

    def tangent_block(blk, _):
        clip = blk // 4
        rows = pl.ds(mult(blk * BLK, BLK), BLK)
        keys = pl.ds(mult(clip * FULL, FULL), FULL)
        query = jnp.concatenate([qkv_d[rows, 0:HD], qkv_s[rows, 0:HD]], axis=1)
        key = jnp.concatenate([qkv_s[keys, HD:2 * HD], qkv_d[keys, HD:2 * HD]], axis=1)
        dscore = lax.dot_general(query, key, NT, preferred_element_type=F32)
        prob = scaled[rows]
        mean = jnp.sum(prob * dscore, axis=-1, keepdims=True) * (1.0 / SCALE)
        dprob = (prob * (dscore - mean)).astype(BF16)
        out = jnp.dot(dprob, qkv_s[keys, 2 * HD:], preferred_element_type=F32)
        out += jnp.dot(weights[rows], qkv_d[keys, 2 * HD:], preferred_element_type=F32)
        mixed_d[rows] = out.astype(BF16)
        send_block(blk, 2, mixed_d, attn_d)
        return 0

    def output(attn, out):
        def tile(n, _):
            cols = pl.ds(mult(n * 512, 512), 512)
            out[:, cols] = jnp.dot(
                attn[...], wo[:, cols], preferred_element_type=F32).astype(BF16)
            return 0

        lax.fori_loop(0, 3, tile, 0)

    arrived(*hop_q)
    for copy in own_q:
        copy.wait()
    rq.step1()
    gx.step1()
    gx.step2()
    rq.step(2)
    gx.step3()
    rq.step(3)
    gx.step4()
    rq.step4()
    arrived(hop_o)
    own_o.wait()
    gx.step5()
    rq.last()
    ro.step1()
    rq.end()

    def early(clip, _):
        base = clip * HALF
        chunk(base, clip * 3, qkv_t, other_t)
        chunk(base, clip * 3 + 1, qkv_s, other_s)
        return 0

    def late_teacher(clip, _):
        chunk(clip * HALF + BLK, clip * 3, qkv_t, other_t)
        return 0

    def late_student(clip, _):
        chunk(clip * HALF + BLK, clip * 3 + 1, qkv_s, other_s)
        return 0

    lax.fori_loop(0, 2, early, 0)
    swaps_t = [exchange(clip, 0, qkv_t, other_t) for clip in range(2)]
    swaps_s = [exchange(clip, 0, qkv_s, other_s) for clip in range(2)]
    gx.end_a()
    gx.end_b()
    lax.fori_loop(0, 2, late_teacher, 0)
    swaps_t += [exchange(clip, 1, qkv_t, other_t) for clip in range(2)]
    lax.fori_loop(0, 2, late_student, 0)
    swaps_s += [exchange(clip, 1, qkv_s, other_s) for clip in range(2)]
    ro.step(2)
    arrived(*swaps_t)
    lax.fori_loop(0, 8, teacher_block, 0)
    ro.step(3)
    arrived(*swaps_s)
    lax.fori_loop(0, 8, student_block, 0)
    ro.step4()
    all_received(0, attn_t)

    def send_student(blk, _):
        send_block(blk, 1, mixed_s, attn_s)
        return 0

    lax.fori_loop(0, 8, send_student, 0)
    ro.last()
    ro.end()
    output(attn_t, vel)

    def dh_piece(i, _):
        rows = pl.ds(mult(i * 32, 32), 32)
        clip = i // 2
        xf = x_ref[rows].astype(F32)
        vf = vel[rows].astype(F32)
        rstd = lax.rsqrt(jnp.mean(xf * xf, axis=-1, keepdims=True) + 1e-6)
        cross = jnp.mean(xf * vf, axis=-1, keepdims=True)
        dnormed = rstd * vf - xf * (rstd * rstd * rstd * cross)
        gain = gains[pl.ds(clip * 3 + 1, 1)]
        dgain = gains[pl.ds(clip * 3 + 2, 1)]
        dh[rows] = (dnormed * gain + xf * rstd * dgain).astype(BF16)
        return 0

    lax.fori_loop(0, 4, dh_piece, 0)
    gd = Gather(dh, dg)
    gd.begin()
    all_received(1, attn_s)
    gd.step1()
    gd.step2()
    gd.step3()
    gd.step4()
    output(attn_s, student_ref)
    gd.step5()

    def early_tangent(clip, _):
        base = mult(clip * HALF, BLK)
        project(dg[pl.ds(base, BLK)], base, qkv_d, other_d)
        return 0

    def late_tangent(clip, _):
        base = mult(clip * HALF + BLK, BLK)
        project(dg[pl.ds(base, BLK)], base, qkv_d, other_d)
        return 0

    lax.fori_loop(0, 2, early_tangent, 0)
    swaps_d = [exchange(clip, 0, qkv_d, other_d) for clip in range(2)]
    gd.end_a()
    gd.end_b()
    lax.fori_loop(0, 2, late_tangent, 0)
    swaps_d += [exchange(clip, 1, qkv_d, other_d) for clip in range(2)]
    arrived(*swaps_d)
    lax.fori_loop(0, 8, tangent_block, 0)
    all_received(2, attn_d)
    output(attn_d, tangent_ref)

    for copy in started:
        copy.wait_send()
    for phase, attn in enumerate((attn_t, attn_s, attn_d)):
        all_sent(phase, attn)


def on_device(x_t, clip_len, time_idx, teacher_mod, student_mod, w_qkv, w_out):
    vmem = pl.BlockSpec(memory_space=pltpu.VMEM)
    smem = pl.BlockSpec(memory_space=pltpu.SMEM)
    hbm = pl.BlockSpec(memory_space=pl.ANY)
    rows = CLIPS * SEG
    out = jax.ShapeDtypeStruct((rows, D), BF16)

    def buf(*shape, dtype=BF16):
        return pltpu.VMEM(shape, dtype)

    scratch = [
        buf(CLIPS * HALF, D), buf(CLIPS * HALF, D), buf(D, 768), buf(INNER, D),
        buf(CLIPS * FULL, 384), buf(CLIPS * FULL, 384), buf(CLIPS * FULL, 384),
        buf(CLIPS * HALF, 384), buf(CLIPS * HALF, 384), buf(CLIPS * HALF, 384),
        buf(BLK, D), buf(8, D, dtype=F32), buf(CLIPS * FULL, HD),
        buf(CLIPS * FULL, HD), buf(CLIPS * FULL, HD), buf(CLIPS * FULL, HD),
        buf(rows, INNER), buf(rows, INNER), buf(rows, INNER),
        buf(rows, D), buf(rows, D),
        buf(CLIPS * FULL, FULL, dtype=F32), buf(CLIPS * FULL, FULL),
        pltpu.SemaphoreType.DMA((96,)), pltpu.SemaphoreType.DMA((96,)),
        pltpu.SemaphoreType.DMA((8,)), pltpu.SemaphoreType.DMA((3,)), pltpu.SemaphoreType.DMA((3,)),
    ]
    student, tangent = pl.pallas_call(
        kernel,
        out_shape=(out, out),
        in_specs=[smem, smem, vmem, vmem, vmem, hbm, hbm],
        out_specs=(vmem, vmem),
        scratch_shapes=scratch,
        compiler_params=pltpu.CompilerParams(
            collective_id=0, has_side_effects=True, vmem_limit_bytes=60 * 2**20),
    )(clip_len, time_idx, x_t.reshape(rows, D), teacher_mod, student_mod, w_qkv, w_out)
    return (student.reshape(CLIPS, SEG, D), tangent.reshape(CLIPS, SEG, D))


def solution(mesh):
    in_specs = (
        P("fsdp", "ctx", None), P("fsdp"), P("fsdp"), P(), P(), P("fsdp", None), P("fsdp", None),
    )
    out_specs = (P("fsdp", "ctx", None), P("fsdp", "ctx", None))
    return jax.shard_map(
        on_device, mesh=mesh, in_specs=in_specs, out_specs=out_specs, check_vma=False)
```

time: 533 us -> 126 us (0.24)
  waiting for transfers between devices: 403 us -> 0 us
  Pallas kernels: 0 us -> 122 us
  matrix products: 51.6 us -> 0 us
  starting transfers between devices: 24.7 us -> 0 us
  local copies, waits for them, and re-layouts: 18 us -> 3.53 us
  blocking collectives: 13.7 us -> 0 us
  between operations: 14.3 us -> 0.64 us
  other arithmetic: 7.49 us -> 0 us
    all_gather x2 -> x0, waiting for transfers between devices: 321 us -> none  [the longest x1 250 us: on_device(): lax.all_gather(w_qkv, 'fsdp', axis=0, tiled=True)]
    pallas_call x0 -> x1, Pallas kernels: none -> 122 us  [on_device(): pl.pallas_call(kernel, out_shape=(out, out), in_specs=[smem, smem, vmem,...]
    all_to_all x5 -> x0, waiting for transfers between devices: 79.8 us -> none  [the longest x1 21.5 us: on_device(): lax.all_to_all(packed_tangent, 'ctx', split_axis=3, concat_axis=1, tiled=...]
    dot_general x20 -> x0, matrix products: 51.6 us -> none  [the longest x1 11.8 us: on_device(): jnp.dot(stacked, qkv_full, preferred_element_type=jnp.float32)]
    all_to_all x5 -> x0, starting transfers between devices: 24.6 us -> none  [the longest x1 5.88 us: on_device(): lax.all_to_all(packed_student, 'ctx', split_axis=3, concat_axis=1, tiled=...]
    all_to_all x1 -> x0, blocking collectives: 13.7 us -> none  [on_device(): lax.all_to_all(mixed_teacher, 'ctx', split_axis=1, concat_axis=2, tiled=T...]
  transfers between devices with their start and end apart: 7 -> 0, of which waited for: 7 -> 0; matrix products, arithmetic and copies ran while one was open for 5% -> 0% of each run, Pallas kernels for 0% -> 0%
where the time goes in v1:
time: 126 us
  Pallas kernels  122 us (97%)
  local copies, waits for them, and re-layouts  3.53 us (3%)
    pallas_call x1, Pallas kernels, on_device(): pl.pallas_call(kernel, out_shape=(out, out), in_specs=[smem, smem, vmem,...  122 us
    unnamed x2, local copies, waits for them, and re-layouts  3.53 us

profile of v1, /device:TPU:1, one launch (start us, length us, event | category | flops | bytes accessed | tf_op | source)
XLA Modules:
  0.0 125.7 jit_solution(1569332356063378234)
XLA Ops:
  0.6 121.5 %shard_map.86 = (bf16[128,1536]{1,0:T(8,128)(2,1)}, bf16[128,1536]{1,0:T(8,128)(2,1)}) custom-call(s32[2]{0:T(128)} %len_ref.1, s32[2]{0:T(128)} %time_ref.1, bf16[128,1536]{1,0:T(8,128)(2,1)} %bitcast.3, f32[2,1536]{1,0:T(2,128)} %tmod_ref.1, f32[2,1536]{1,0:T(2,128)} %smod_ref.1, bf16[96,6144]{1,0:T(8,128)(2,1)} %wqkv_ref.1, bf16[128,1536]{1,0:T(8,128)(2,1)} %wout_ref.1), custom_call_target="tpu_custom_call" | custom-call | tf_op jit(solution)/shard_map/pallas_call | solution.py:487
  122.2 1.8 %copy.11 = bf16[2,64,1536]{2,1,0:T(8,128)(2,1)} copy(bf16[2,64,1536]{2,1,0:T(8,128)(2,1)} %bitcast.5) | data formatting | bytes 786432
  124.0 1.8 %copy.12 = bf16[2,64,1536]{2,1,0:T(8,128)(2,1)} copy(bf16[2,64,1536]{2,1,0:T(8,128)(2,1)} %bitcast.4) | data formatting | bytes 786432

commit v2 on v1

--- a/solution.py
+++ b/solution.py
@@ -28,6 +28,9 @@
 S00, S01, S03, S10, S02, S11, S13, S12 = range(8)
 
 
+PLACES = ((0, 0), (0, 1), (0, 3), (1, 0), (0, 2), (1, 1), (1, 3), (1, 2))
+
+
 def mult(value, by):
     return pl.multiple_of(value, by)
 
@@ -35,8 +38,9 @@
 def kernel(
     len_ref, time_ref, x_ref, tmod_ref, smod_ref, wqkv_ref, wout_ref,
     student_ref, tangent_ref,
-    xg, dg, wq, wo, qkv_t, qkv_s, qkv_d, other_t, other_s, other_d, hbuf, gains, kmask,
+    xg, dg, wq, wo, qkv_t, qkv_s, qkv_d, other_t, other_s, other_d, h_t, h_s, gains, kmask,
     mixed_t, mixed_s, mixed_d, attn_t, attn_s, attn_d, vel, dh, scaled, weights,
+    score0, score1, weigh0, weigh1, total0, total1,
     send, recv, local, bulk_send, bulk_recv,
 ):
     c = lax.axis_index("ctx")
@@ -152,21 +156,19 @@
         def end_b(self):
             arrived(self.b_y1, self.b_y3, self.b_y2)
 
-    class Ring:
-        def __init__(self, buf, rows, cols, core_cols):
-            self.buf, self.rows, self.cols, self.core_cols = buf, rows, cols, core_cols
+    class Chain:
+        def __init__(self, buf, rows, part, cols, core_cols):
+            self.buf, self.rows, self.part = buf, rows, part
+            self.cols, self.core_cols = cols, core_cols
             self.cores = []
 
-        def block(self, dz, part=None):
-            base = mult((z + dz) % 8 * (2 * self.rows), 16)
-            if part is None:
-                return self.buf.at[pl.ds(base, 2 * self.rows), self.cols]
-            return self.buf.at[pl.ds(base + part * self.rows, self.rows), self.cols]
+        def block(self, dz, lo=0, n=None, cols=None):
+            base = mult(((z + dz) % 8 * 2 + self.part) * self.rows + lo, 16)
+            return self.buf.at[pl.ds(base, n or self.rows), self.cols if cols is None else cols]
 
         def share(self, dz):
-            base = mult((z + dz) % 8 * (2 * self.rows), 16)
             self.cores.append(remote(
-                self.block(dz), self.buf.at[pl.ds(base, 2 * self.rows), self.core_cols], sibling))
+                self.block(dz), self.block(dz, cols=self.core_cols), sibling))
 
         def step1(self):
             self.up = remote(self.block(0), self.block(0), z_up)
@@ -174,22 +176,15 @@
             self.share(0)
 
         def step(self, k):
+            half = self.rows // 2
             arrived(self.up)
-            if k < 4:
-                self.up = remote(self.block(-k + 1), self.block(-k + 1), z_up)
+            lo, n = (0, half) if k == 4 else (0, self.rows)
+            self.up = remote(self.block(9 - k, lo, n), self.block(9 - k, lo, n), z_up)
             arrived(self.down)
-            if k < 4:
-                self.down = remote(self.block(k - 1), self.block(k - 1), z_down)
-            self.share(8 - k + 1)
+            lo, n = (half, half) if k == 4 else (0, self.rows)
+            self.down = remote(self.block(k - 1, lo, n), self.block(k - 1, lo, n), z_down)
+            self.share(9 - k)
             self.share(k - 1)
-
-        def step4(self):
-            arrived(self.up)
-            self.up = remote(self.block(-3, 0), self.block(-3, 0), z_up)
-            arrived(self.down)
-            self.down = remote(self.block(3, 1), self.block(3, 1), z_down)
-            self.share(5)
-            self.share(3)
 
         def last(self):
             arrived(self.up, self.down)
@@ -198,18 +193,8 @@
         def end(self):
             arrived(*self.cores)
 
-    pl.semaphore_wait(barrier, len(partners))
-
-    gx = Gather(x_ref, xg)
-    gx.begin()
     c_out = (c + 8) % 16
     row_q = mult(f * 96, 16)
-    hop_q = [
-        remote(
-            wqkv_ref.at[:, pl.ds(mult(part * INNER + c_out * HD, HD), HD)],
-            wq.at[pl.ds(row_q, 96), pl.ds(part * HD, HD)], y_out)
-        for part in range(3)
-    ]
     own_q = [
         here(
             wqkv_ref.at[:, pl.ds(mult(part * INNER + c * HD, HD), HD)],
@@ -218,10 +203,12 @@
     ]
     my_cols = pl.ds(mult(core * 768, HD), 768)
     row_o = mult(f * HD, HD)
-    hop_o = remote(wout_ref.at[:, my_cols], wo.at[pl.ds(row_o, HD), my_cols], y_out)
     own_o = here(wout_ref.at[:, my_cols], wo.at[pl.ds(row_o, HD), my_cols])
-    rq = Ring(wq, 96, pl.ds(0, 384), pl.ds(384, 384))
-    ro = Ring(wo, HD, my_cols, my_cols)
+    gx = Gather(x_ref, xg)
+    qa = Chain(wq, 96, yh, pl.ds(0, 384), pl.ds(384, 384))
+    qb = Chain(wq, 96, 1 - yh, pl.ds(0, 384), pl.ds(384, 384))
+    oa = Chain(wo, HD, yh, my_cols, my_cols)
+    ob = Chain(wo, HD, 1 - yh, my_cols, my_cols)
 
     for clip in range(CLIPS):
         angle = jnp.full((1, D), time_ref[clip].astype(F32), F32)
@@ -232,31 +219,34 @@
         gains[pl.ds(clip * 3 + 2, 1)] = cos_t * smod_ref[0:1] - sin_t * smod_ref[1:2]
     within = lax.broadcasted_iota(jnp.int32, (SEG, HD), 0)
     lane0 = lax.broadcasted_iota(jnp.int32, (SEG, HD), 1) == 0
-    places = ((0, 0), (0, 1), (0, 3), (1, 0), (0, 2), (1, 1), (1, 3), (1, 2))
     for clip in range(CLIPS):
         for half in range(2):
-            for slot, (dyl, dx) in enumerate(places):
+            for slot, (dyl, dx) in enumerate(PLACES):
                 token = within + device(dcore=half, dx=dx, dyl=dyl)[0] * SEG
                 dead = jnp.logical_and(token >= len_ref[clip], lane0)
                 kmask[pl.ds(clip * FULL + half * HALF + slot * SEG, SEG)] = jnp.where(
                     dead, -1e30, 0.0).astype(BF16)
-    one0 = jnp.where(lax.broadcasted_iota(jnp.int32, (BLK, HD), 1) == 0, 1.0, 0.0).astype(BF16)
+    one0 = jnp.where(lax.broadcasted_iota(jnp.int32, (HALF, HD), 1) == 0, 1.0, 0.0).astype(BF16)
 
     def project(source, base, out, other):
-        y = jnp.dot(source, wq[...], preferred_element_type=F32).astype(BF16)
+        y = jnp.dot(source[pl.ds(base, BLK)], wq[...], preferred_element_type=F32).astype(BF16)
         clip, rest = base // HALF, base % HALF
         out[pl.ds(mult(clip * FULL + rest, BLK), BLK)] = y[:, :384]
-        other[pl.ds(mult(base, BLK), BLK)] = y[:, 384:]
-
-    def chunk(base, gain_row, out, other):
+        other[pl.ds(base, BLK)] = y[:, 384:]
+
+    def modulate(base):
+        clip = base // HALF
+
         def piece(i, _):
-            xf = xg[pl.ds(mult(base + i * 32, 32), 32)].astype(F32)
+            rows = pl.ds(mult(base + i * 32, 32), 32)
+            xf = xg[rows].astype(F32)
             rstd = lax.rsqrt(jnp.mean(xf * xf, axis=-1, keepdims=True) + 1e-6)
-            hbuf[pl.ds(mult(i * 32, 32), 32)] = (xf * rstd * gains[pl.ds(gain_row, 1)]).astype(BF16)
+            normed = xf * rstd
+            h_t[rows] = (normed * gains[pl.ds(clip * 3, 1)]).astype(BF16)
+            h_s[rows] = (normed * gains[pl.ds(clip * 3 + 1, 1)]).astype(BF16)
             return 0
 
         lax.fori_loop(0, BLK // 32, piece, 0)
-        project(hbuf[...], base, out, other)
 
     def exchange(clip, group, out, other):
         return remote(
@@ -264,31 +254,19 @@
             out.at[pl.ds(clip * FULL + HALF + group * BLK, BLK)], sibling)
 
     def send_block(blk, phase, mixed, attn):
-        clip = blk // 4
-        half = blk // 2 % 2
-        group = blk % 2
-        steps = ((0, 2 * group), (group, 1), (group, 3), (1, 2 * group))
-        for j, (dyl, dx) in enumerate(steps):
-            where = device(dcore=half, dx=dx, dyl=dyl)
-            src = mixed.at[pl.ds(mult(blk * BLK + j * SEG, SEG), SEG)]
-            dst = attn.at[pl.ds(mult(clip * SEG, SEG), SEG), pl.ds(mult(c * HD, HD), HD)]
-
-            def away(src=src, dst=dst, where=where):
+        clip, half = blk // 2, blk % 2
+        for slot in (7, 4, 5, 6, 3, 1, 2, 0):
+            dyl, dx = PLACES[slot]
+            src = mixed.at[pl.ds(blk * HALF + slot * SEG, SEG)]
+            dst = attn.at[pl.ds(clip * SEG, SEG), pl.ds(mult(c * HD, HD), HD)]
+            if half + slot == 0:
+                pltpu.make_async_copy(src, dst, bulk_recv.at[phase]).start()
+            else:
                 pltpu.make_async_remote_copy(
                     src_ref=src, dst_ref=dst, send_sem=bulk_send.at[phase],
-                    recv_sem=bulk_recv.at[phase], device_id=where, device_id_type=MESH,
+                    recv_sem=bulk_recv.at[phase],
+                    device_id=device(dcore=half, dx=dx, dyl=dyl), device_id_type=MESH,
                 ).start()
-
-            if j == 0:
-                stays = half + group == 0
-
-                @pl.when(stays)
-                def _(src=src, dst=dst):
-                    pltpu.make_async_copy(src, dst, bulk_recv.at[phase]).start()
-
-                pl.when(jnp.logical_not(stays))(away)
-            else:
-                away()
 
     def all_received(phase, attn):
         pltpu.make_async_copy(attn, attn, bulk_recv.at[phase]).wait()
@@ -299,49 +277,80 @@
 
     NT = (((1,), (1,)), ((), ()))
 
-    def scores_of(blk, qkv):
-        clip = blk // 4
-        rows = pl.ds(mult(blk * BLK, BLK), BLK)
-        keys = pl.ds(mult(clip * FULL, FULL), FULL)
+    def places_of(blk):
+        return pl.ds(blk * HALF, HALF), pl.ds(blk // 2 * FULL, FULL)
+
+    def masked_scores(blk, qkv, out):
+        rows, keys = places_of(blk)
         query = jnp.concatenate([qkv[rows, 0:HD], one0], axis=1)
         key = jnp.concatenate([qkv[keys, HD:2 * HD], kmask[keys]], axis=1)
-        scores = lax.dot_general(query, key, NT, preferred_element_type=F32)
+        out[...] = lax.dot_general(query, key, NT, preferred_element_type=F32)
+
+    def pipeline(first, second, third):
+        first(0, 0)
+        first(1, 1)
+        second(0, 0)
+        first(2, 0)
+        second(1, 1)
+        third(0, 0)
+        first(3, 1)
+        second(2, 0)
+        third(1, 1)
+        second(3, 1)
+        third(2, 0)
+        third(3, 1)
+
+    score = (score0, score1)
+    weigh = (weigh0, weigh1)
+    totals = (total0, total1)
+
+    def teacher_scores(blk, p):
+        masked_scores(blk, qkv_t, score[p])
+
+    def teacher_softmax(blk, p):
+        scores = score[p][...]
         top = jnp.max(scores, axis=-1, keepdims=True)
         expo = jnp.exp2((scores - top) * EXP2_SCALE)
-        return rows, keys, expo, jnp.sum(expo, axis=-1, keepdims=True)
-
-    def teacher_block(blk, _):
-        rows, keys, expo, total = scores_of(blk, qkv_t)
-        out = jnp.dot(expo.astype(BF16), qkv_t[keys, 2 * HD:], preferred_element_type=F32)
-        mixed_t[rows] = (out / total).astype(BF16)
+        totals[p][...] = jnp.broadcast_to(jnp.sum(expo, axis=-1, keepdims=True), (HALF, HD))
+        weigh[p][...] = expo.astype(BF16)
+
+    def teacher_values(blk, p):
+        rows, keys = places_of(blk)
+        out = jnp.dot(weigh[p][...], qkv_t[keys, 2 * HD:], preferred_element_type=F32)
+        mixed_t[rows] = (out / totals[p][...]).astype(BF16)
         send_block(blk, 0, mixed_t, attn_t)
-        return 0
-
-    def student_block(blk, _):
-        rows, keys, expo, total = scores_of(blk, qkv_s)
-        probs = expo * (1.0 / total)
-        weight = probs.astype(BF16)
-        weights[rows] = weight
+
+    def student_block(blk):
+        rows, keys = places_of(blk)
+        masked_scores(blk, qkv_s, score[0])
+        scores = score[0][...]
+        top = jnp.max(scores, axis=-1, keepdims=True)
+        expo = jnp.exp2((scores - top) * EXP2_SCALE)
+        probs = expo * (1.0 / jnp.sum(expo, axis=-1, keepdims=True))
+        weights[rows] = probs.astype(BF16)
         scaled[rows] = probs * SCALE
         mixed_s[rows] = jnp.dot(
-            weight, qkv_s[keys, 2 * HD:], preferred_element_type=F32).astype(BF16)
-        return 0
-
-    def tangent_block(blk, _):
-        clip = blk // 4
-        rows = pl.ds(mult(blk * BLK, BLK), BLK)
-        keys = pl.ds(mult(clip * FULL, FULL), FULL)
+            weights[rows], qkv_s[keys, 2 * HD:], preferred_element_type=F32).astype(BF16)
+
+    def tangent_scores(blk, p):
+        rows, keys = places_of(blk)
         query = jnp.concatenate([qkv_d[rows, 0:HD], qkv_s[rows, 0:HD]], axis=1)
         key = jnp.concatenate([qkv_s[keys, HD:2 * HD], qkv_d[keys, HD:2 * HD]], axis=1)
-        dscore = lax.dot_general(query, key, NT, preferred_element_type=F32)
+        score[p][...] = lax.dot_general(query, key, NT, preferred_element_type=F32)
+
+    def tangent_probs(blk, p):
+        rows, keys = places_of(blk)
+        dscore = score[p][...]
         prob = scaled[rows]
         mean = jnp.sum(prob * dscore, axis=-1, keepdims=True) * (1.0 / SCALE)
-        dprob = (prob * (dscore - mean)).astype(BF16)
-        out = jnp.dot(dprob, qkv_s[keys, 2 * HD:], preferred_element_type=F32)
+        weigh[p][...] = (prob * (dscore - mean)).astype(BF16)
+
+    def tangent_values(blk, p):
+        rows, keys = places_of(blk)
+        out = jnp.dot(weigh[p][...], qkv_s[keys, 2 * HD:], preferred_element_type=F32)
         out += jnp.dot(weights[rows], qkv_d[keys, 2 * HD:], preferred_element_type=F32)
         mixed_d[rows] = out.astype(BF16)
         send_block(blk, 2, mixed_d, attn_d)
-        return 0
 
     def output(attn, out):
         def tile(n, _):
@@ -352,63 +361,74 @@
 
         lax.fori_loop(0, 3, tile, 0)
 
-    arrived(*hop_q)
     for copy in own_q:
         copy.wait()
-    rq.step1()
+    own_o.wait()
+    pl.semaphore_wait(barrier, len(partners))
+
+    qa.step1()
+    hop_q = [
+        remote(
+            wqkv_ref.at[:, pl.ds(mult(part * INNER + c_out * HD, HD), HD)],
+            wq.at[pl.ds(row_q, 96), pl.ds(part * HD, HD)], y_out)
+        for part in range(3)
+    ]
+    gx.begin()
+    hop_o = remote(wo.at[pl.ds(row_o, HD), my_cols], wo.at[pl.ds(row_o, HD), my_cols], y_out)
+    arrived(*hop_q)
+    qb.step1()
+    qa.step(2)
     gx.step1()
+    qb.step(2)
     gx.step2()
-    rq.step(2)
+    qa.step(3)
     gx.step3()
-    rq.step(3)
+    qb.step(3)
+    qa.step(4)
+    oa.step1()
     gx.step4()
-    rq.step4()
+    qb.step(4)
     arrived(hop_o)
-    own_o.wait()
+    ob.step1()
+    qa.last()
+
+    modulate(0)
     gx.step5()
-    rq.last()
-    ro.step1()
-    rq.end()
-
-    def early(clip, _):
-        base = clip * HALF
-        chunk(base, clip * 3, qkv_t, other_t)
-        chunk(base, clip * 3 + 1, qkv_s, other_s)
-        return 0
-
-    def late_teacher(clip, _):
-        chunk(clip * HALF + BLK, clip * 3, qkv_t, other_t)
-        return 0
-
-    def late_student(clip, _):
-        chunk(clip * HALF + BLK, clip * 3 + 1, qkv_s, other_s)
-        return 0
-
-    lax.fori_loop(0, 2, early, 0)
+    qb.last()
+    modulate(HALF)
+    oa.step(2)
+    qa.end()
+    qb.end()
+    project(h_t, 0, qkv_t, other_t)
+    project(h_t, HALF, qkv_t, other_t)
     swaps_t = [exchange(clip, 0, qkv_t, other_t) for clip in range(2)]
+    ob.step(2)
+    project(h_s, 0, qkv_s, other_s)
+    project(h_s, HALF, qkv_s, other_s)
     swaps_s = [exchange(clip, 0, qkv_s, other_s) for clip in range(2)]
     gx.end_a()
+    modulate(BLK)
+    project(h_t, BLK, qkv_t, other_t)
+    swaps_t.append(exchange(0, 1, qkv_t, other_t))
+    oa.step(3)
     gx.end_b()
-    lax.fori_loop(0, 2, late_teacher, 0)
-    swaps_t += [exchange(clip, 1, qkv_t, other_t) for clip in range(2)]
-    lax.fori_loop(0, 2, late_student, 0)
-    swaps_s += [exchange(clip, 1, qkv_s, other_s) for clip in range(2)]
-    ro.step(2)
+    modulate(HALF + BLK)
+    project(h_t, HALF + BLK, qkv_t, other_t)
+    swaps_t.append(exchange(1, 1, qkv_t, other_t))
+    project(h_s, BLK, qkv_s, other_s)
+    swaps_s.append(exchange(0, 1, qkv_s, other_s))
     arrived(*swaps_t)
-    lax.fori_loop(0, 8, teacher_block, 0)
-    ro.step(3)
-    arrived(*swaps_s)
-    lax.fori_loop(0, 8, student_block, 0)
-    ro.step4()
+    ob.step(3)
+    pipeline(teacher_scores, teacher_softmax, teacher_values)
+    oa.step(4)
+    project(h_s, HALF + BLK, qkv_s, other_s)
+    swaps_s.append(exchange(1, 1, qkv_s, other_s))
+    ob.step(4)
     all_received(0, attn_t)
-
-    def send_student(blk, _):
-        send_block(blk, 1, mixed_s, attn_s)
-        return 0
-
-    lax.fori_loop(0, 8, send_student, 0)
-    ro.last()
-    ro.end()
+    oa.last()
+    ob.last()
+    oa.end()
+    ob.end()
     output(attn_t, vel)
 
     def dh_piece(i, _):
@@ -427,32 +447,31 @@
     lax.fori_loop(0, 4, dh_piece, 0)
     gd = Gather(dh, dg)
     gd.begin()
-    all_received(1, attn_s)
+    arrived(*swaps_s)
+    student_block(0)
     gd.step1()
     gd.step2()
+    student_block(1)
+    student_block(2)
     gd.step3()
+    student_block(3)
     gd.step4()
-    output(attn_s, student_ref)
     gd.step5()
-
-    def early_tangent(clip, _):
-        base = mult(clip * HALF, BLK)
-        project(dg[pl.ds(base, BLK)], base, qkv_d, other_d)
-        return 0
-
-    def late_tangent(clip, _):
-        base = mult(clip * HALF + BLK, BLK)
-        project(dg[pl.ds(base, BLK)], base, qkv_d, other_d)
-        return 0
-
-    lax.fori_loop(0, 2, early_tangent, 0)
+    project(dg, 0, qkv_d, other_d)
+    project(dg, HALF, qkv_d, other_d)
     swaps_d = [exchange(clip, 0, qkv_d, other_d) for clip in range(2)]
     gd.end_a()
+    project(dg, BLK, qkv_d, other_d)
+    swaps_d.append(exchange(0, 1, qkv_d, other_d))
     gd.end_b()
-    lax.fori_loop(0, 2, late_tangent, 0)
-    swaps_d += [exchange(clip, 1, qkv_d, other_d) for clip in range(2)]
+    project(dg, HALF + BLK, qkv_d, other_d)
+    swaps_d.append(exchange(1, 1, qkv_d, other_d))
+    for blk in range(4):
+        send_block(blk, 1, mixed_s, attn_s)
     arrived(*swaps_d)
-    lax.fori_loop(0, 8, tangent_block, 0)
+    pipeline(tangent_scores, tangent_probs, tangent_values)
+    all_received(1, attn_s)
+    output(attn_s, student_ref)
     all_received(2, attn_d)
     output(attn_d, tangent_ref)
 
@@ -476,12 +495,14 @@
         buf(CLIPS * HALF, D), buf(CLIPS * HALF, D), buf(D, 768), buf(INNER, D),
         buf(CLIPS * FULL, 384), buf(CLIPS * FULL, 384), buf(CLIPS * FULL, 384),
         buf(CLIPS * HALF, 384), buf(CLIPS * HALF, 384), buf(CLIPS * HALF, 384),
-        buf(BLK, D), buf(8, D, dtype=F32), buf(CLIPS * FULL, HD),
+        buf(CLIPS * HALF, D), buf(CLIPS * HALF, D), buf(8, D, dtype=F32), buf(CLIPS * FULL, HD),
         buf(CLIPS * FULL, HD), buf(CLIPS * FULL, HD), buf(CLIPS * FULL, HD),
         buf(rows, INNER), buf(rows, INNER), buf(rows, INNER),
         buf(rows, D), buf(rows, D),
         buf(CLIPS * FULL, FULL, dtype=F32), buf(CLIPS * FULL, FULL),
-        pltpu.SemaphoreType.DMA((96,)), pltpu.SemaphoreType.DMA((96,)),
+        buf(HALF, FULL, dtype=F32), buf(HALF, FULL, dtype=F32), buf(HALF, FULL), buf(HALF, FULL),
+        buf(HALF, HD, dtype=F32), buf(HALF, HD, dtype=F32),
+        pltpu.SemaphoreType.DMA((128,)), pltpu.SemaphoreType.DMA((128,)),
         pltpu.SemaphoreType.DMA((8,)), pltpu.SemaphoreType.DMA((3,)), pltpu.SemaphoreType.DMA((3,)),
     ]
     student, tangent = pl.pallas_call(

time: 126 us -> 107 us (0.85)
  Pallas kernels: 122 us -> 102 us
    pallas_call x1, Pallas kernels: 122 us -> 102 us  [on_device(): pl.pallas_call(kernel, out_shape=(out, out), in_specs=[smem, smem, vmem,...]
where the time goes in v2:
time: 107 us
  Pallas kernels  102 us (95%)
  local copies, waits for them, and re-layouts  3.53 us (3%)
    pallas_call x1, Pallas kernels, on_device(): pl.pallas_call(kernel, out_shape=(out, out), in_specs=[smem, smem, vmem,...  102 us
    unnamed x2, local copies, waits for them, and re-layouts  3.53 us

profile of v2, /device:TPU:1, one launch (start us, length us, event | category | flops | bytes accessed | tf_op | source)
XLA Modules:
  0.0 106.5 jit_solution(11458911951169068936)
XLA Ops:
  0.6 102.4 %shard_map.86 = (bf16[128,1536]{1,0:T(8,128)(2,1)}, bf16[128,1536]{1,0:T(8,128)(2,1)}) custom-call(s32[2]{0:T(128)} %len_ref.1, s32[2]{0:T(128)} %time_ref.1, bf16[128,1536]{1,0:T(8,128)(2,1)} %bitcast.3, f32[2,1536]{1,0:T(2,128)} %tmod_ref.1, f32[2,1536]{1,0:T(2,128)} %smod_ref.1, bf16[96,6144]{1,0:T(8,128)(2,1)} %wqkv_ref.1, bf16[128,1536]{1,0:T(8,128)(2,1)} %wout_ref.1), custom_call_target="tpu_custom_call" | custom-call | tf_op jit(solution)/shard_map/pallas_call | solution.py:508
  103.0 1.8 %copy.11 = bf16[2,64,1536]{2,1,0:T(8,128)(2,1)} copy(bf16[2,64,1536]{2,1,0:T(8,128)(2,1)} %bitcast.5) | data formatting | bytes 786432
  104.8 1.8 %copy.12 = bf16[2,64,1536]{2,1,0:T(8,128)(2,1)} copy(bf16[2,64,1536]{2,1,0:T(8,128)(2,1)} %bitcast.4) | data formatting | bytes 786432

commit v3 on v2

--- a/solution.py
+++ b/solution.py
@@ -25,6 +25,8 @@
 F32 = jnp.float32
 BF16 = jnp.bfloat16
 
+RING = 256
+
 S00, S01, S03, S10, S02, S11, S13, S12 = range(8)
 
 
@@ -52,23 +54,25 @@
     z = f // 2
     yh = f % 2
 
-    def device(dcore=0, dx=0, dyl=0, dz=0, dyh=0):
-        ctx = ((yl + dyl) % 2 * 4 + (xx + dx) % 4) * 2 + (core + dcore) % 2
-        return (ctx, (z + dz) % 8 * 2 + (yh + dyh) % 2)
-
-    sibling = device(dcore=1)
-    x_up, x_down = device(dx=1), device(dx=3)
-    y_in = device(dyl=1)
-    y_out = device(dyl=1, dyh=1)
-    z_up, z_down = device(dz=1), device(dz=7)
+    chips = [((yl + dyl) % 2 * 4 + (xx + dx) % 4) * 2 for dyl, dx in PLACES]
+    halves = (core, 1 - core)
+    columns = [(z + dz) % 8 * 2 for dz in range(8)]
+
+    def member(slot, half):
+        return chips[slot] + halves[half]
+
+    sibling = (member(S00, 1), f)
+    x_up, x_down = (member(S01, 0), f), (member(S03, 0), f)
+    y_in = (member(S10, 0), f)
+    y_out = (member(S10, 0), columns[0] + 1 - yh)
+    z_up, z_down = (c, columns[1] + yh), (c, columns[7] + yh)
 
     barrier = pltpu.get_barrier_semaphore()
     partners = [y_out, z_up, z_down]
-    for dyl in range(2):
-        for dx in range(4):
-            for dcore in range(2):
-                if dyl + dx + dcore:
-                    partners.append(device(dcore=dcore, dx=dx, dyl=dyl))
+    for slot in range(SLOTS):
+        for half in range(2):
+            if slot + half:
+                partners.append((member(slot, half), f))
     for partner in partners:
         pl.semaphore_signal(barrier, inc=1, device_id=partner, device_id_type=MESH)
 
@@ -157,14 +161,16 @@
             arrived(self.b_y1, self.b_y3, self.b_y2)
 
     class Chain:
-        def __init__(self, buf, rows, part, cols, core_cols):
+        def __init__(self, buf, rows, part, cols, core_cols, first=0, count=None):
             self.buf, self.rows, self.part = buf, rows, part
+            self.first, self.count = first, count or rows
             self.cols, self.core_cols = cols, core_cols
             self.cores = []
 
-        def block(self, dz, lo=0, n=None, cols=None):
-            base = mult(((z + dz) % 8 * 2 + self.part) * self.rows + lo, 16)
-            return self.buf.at[pl.ds(base, n or self.rows), self.cols if cols is None else cols]
+        def block(self, dz, lo=0, n=None, cols=None, part=None):
+            at = columns[dz % 8] + (self.part if part is None else part)
+            base = mult(at * self.rows + self.first + lo, 16)
+            return self.buf.at[pl.ds(base, n or self.count), self.cols if cols is None else cols]
 
         def share(self, dz):
             self.cores.append(remote(
@@ -176,12 +182,12 @@
             self.share(0)
 
         def step(self, k):
-            half = self.rows // 2
+            half = self.count // 2
             arrived(self.up)
-            lo, n = (0, half) if k == 4 else (0, self.rows)
+            lo, n = (0, half) if k == 4 else (0, self.count)
             self.up = remote(self.block(9 - k, lo, n), self.block(9 - k, lo, n), z_up)
             arrived(self.down)
-            lo, n = (half, half) if k == 4 else (0, self.rows)
+            lo, n = (half, half) if k == 4 else (0, self.count)
             self.down = remote(self.block(k - 1, lo, n), self.block(k - 1, lo, n), z_down)
             self.share(9 - k)
             self.share(k - 1)
@@ -192,6 +198,23 @@
 
         def end(self):
             arrived(*self.cores)
+
+    class WideChain(Chain):
+        def __init__(self, across_cols, *args):
+            super().__init__(*args)
+            self.across_cols, self.across = across_cols, []
+
+        def share(self, dz):
+            across = self.block(dz, cols=self.across_cols)
+            self.across.append((dz, remote(across, across, y_out)))
+            super().share(dz)
+
+        def take(self, leave=0):
+            while len(self.across) > leave:
+                dz, copy = self.across.pop(0)
+                arrived(copy)
+                there = self.block(dz, cols=self.across_cols, part=1 - self.part)
+                self.cores.append(remote(there, there, sibling))
 
     c_out = (c + 8) % 16
     row_q = mult(f * 96, 16)
@@ -207,8 +230,11 @@
     gx = Gather(x_ref, xg)
     qa = Chain(wq, 96, yh, pl.ds(0, 384), pl.ds(384, 384))
     qb = Chain(wq, 96, 1 - yh, pl.ds(0, 384), pl.ds(384, 384))
-    oa = Chain(wo, HD, yh, my_cols, my_cols)
-    ob = Chain(wo, HD, 1 - yh, my_cols, my_cols)
+    ring_cols = pl.ds(mult(core * 768, HD), RING)
+    across_cols = pl.ds(mult(core * 768 + RING, HD), 768 - RING)
+    oa = WideChain(across_cols, wo, HD, yh, my_cols, my_cols, 0, 64)
+    oc = WideChain(across_cols, wo, HD, yh, my_cols, my_cols, 64, 64)
+    ob = Chain(wo, HD, 1 - yh, ring_cols, ring_cols)
 
     for clip in range(CLIPS):
         angle = jnp.full((1, D), time_ref[clip].astype(F32), F32)
@@ -221,8 +247,8 @@
     lane0 = lax.broadcasted_iota(jnp.int32, (SEG, HD), 1) == 0
     for clip in range(CLIPS):
         for half in range(2):
-            for slot, (dyl, dx) in enumerate(PLACES):
-                token = within + device(dcore=half, dx=dx, dyl=dyl)[0] * SEG
+            for slot in range(SLOTS):
+                token = within + member(slot, half) * SEG
                 dead = jnp.logical_and(token >= len_ref[clip], lane0)
                 kmask[pl.ds(clip * FULL + half * HALF + slot * SEG, SEG)] = jnp.where(
                     dead, -1e30, 0.0).astype(BF16)
@@ -256,7 +282,6 @@
     def send_block(blk, phase, mixed, attn):
         clip, half = blk // 2, blk % 2
         for slot in (7, 4, 5, 6, 3, 1, 2, 0):
-            dyl, dx = PLACES[slot]
             src = mixed.at[pl.ds(blk * HALF + slot * SEG, SEG)]
             dst = attn.at[pl.ds(clip * SEG, SEG), pl.ds(mult(c * HD, HD), HD)]
             if half + slot == 0:
@@ -265,7 +290,7 @@
                 pltpu.make_async_remote_copy(
                     src_ref=src, dst_ref=dst, send_sem=bulk_send.at[phase],
                     recv_sem=bulk_recv.at[phase],
-                    device_id=device(dcore=half, dx=dx, dyl=dyl), device_id_type=MESH,
+                    device_id=(member(slot, half), f), device_id_type=MESH,
                 ).start()
 
     def all_received(phase, attn):
@@ -286,16 +311,18 @@
         key = jnp.concatenate([qkv[keys, HD:2 * HD], kmask[keys]], axis=1)
         out[...] = lax.dot_general(query, key, NT, preferred_element_type=F32)
 
-    def pipeline(first, second, third):
+    def pipeline(first, second, third, between=lambda stage: None):
         first(0, 0)
         first(1, 1)
         second(0, 0)
         first(2, 0)
         second(1, 1)
         third(0, 0)
+        between(0)
         first(3, 1)
         second(2, 0)
         third(1, 1)
+        between(1)
         second(3, 1)
         third(2, 0)
         third(3, 1)
@@ -374,60 +401,74 @@
         for part in range(3)
     ]
     gx.begin()
-    hop_o = remote(wo.at[pl.ds(row_o, HD), my_cols], wo.at[pl.ds(row_o, HD), my_cols], y_out)
     arrived(*hop_q)
     qb.step1()
     qa.step(2)
     gx.step1()
+    gx.step2()
     qb.step(2)
-    gx.step2()
+    hop_o = remote(
+        wo.at[pl.ds(row_o, HD), ring_cols], wo.at[pl.ds(row_o, HD), ring_cols], y_out)
     qa.step(3)
+    oa.step1()
     gx.step3()
     qb.step(3)
+    oc.step1()
+    gx.step4()
     qa.step(4)
-    oa.step1()
-    gx.step4()
-    qb.step(4)
     arrived(hop_o)
     ob.step1()
+    qb.step(4)
+    gx.step5()
+    modulate(0)
     qa.last()
-
-    modulate(0)
-    gx.step5()
+    modulate(HALF)
     qb.last()
-    modulate(HALF)
     oa.step(2)
+    oc.step(2)
     qa.end()
     qb.end()
+
     project(h_t, 0, qkv_t, other_t)
     project(h_t, HALF, qkv_t, other_t)
     swaps_t = [exchange(clip, 0, qkv_t, other_t) for clip in range(2)]
     ob.step(2)
-    project(h_s, 0, qkv_s, other_s)
-    project(h_s, HALF, qkv_s, other_s)
-    swaps_s = [exchange(clip, 0, qkv_s, other_s) for clip in range(2)]
     gx.end_a()
     modulate(BLK)
     project(h_t, BLK, qkv_t, other_t)
     swaps_t.append(exchange(0, 1, qkv_t, other_t))
-    oa.step(3)
     gx.end_b()
     modulate(HALF + BLK)
     project(h_t, HALF + BLK, qkv_t, other_t)
     swaps_t.append(exchange(1, 1, qkv_t, other_t))
+    oa.step(3)
+    oc.step(3)
+    project(h_s, 0, qkv_s, other_s)
+    swaps_s = [exchange(0, 0, qkv_s, other_s)]
+    arrived(*swaps_t)
+
+    def between(stage):
+        if stage == 0:
+            ob.step(3)
+            oa.step(4)
+        if stage == 1:
+            oc.step(4)
+
+    pipeline(teacher_scores, teacher_softmax, teacher_values, between)
+    ob.step(4)
+    project(h_s, HALF, qkv_s, other_s)
+    swaps_s.append(exchange(1, 0, qkv_s, other_s))
+    oa.last()
     project(h_s, BLK, qkv_s, other_s)
-    swaps_s.append(exchange(0, 1, qkv_s, other_s))
-    arrived(*swaps_t)
-    ob.step(3)
-    pipeline(teacher_scores, teacher_softmax, teacher_values)
-    oa.step(4)
+    oc.last()
     project(h_s, HALF + BLK, qkv_s, other_s)
-    swaps_s.append(exchange(1, 1, qkv_s, other_s))
-    ob.step(4)
+    swaps_s += [exchange(clip, 1, qkv_s, other_s) for clip in range(2)]
+    ob.last()
+    oa.take()
+    oc.take()
     all_received(0, attn_t)
-    oa.last()
-    ob.last()
     oa.end()
+    oc.end()
     ob.end()
     output(attn_t, vel)
 
@@ -481,6 +522,11 @@
         all_sent(phase, attn)
 
 
+def hand_over(student_ref, tangent_ref, student_out, tangent_out):
+    student_out[...] = student_ref[...]
+    tangent_out[...] = tangent_ref[...]
+
+
 def on_device(x_t, clip_len, time_idx, teacher_mod, student_mod, w_qkv, w_out):
     vmem = pl.BlockSpec(memory_space=pltpu.VMEM)
     smem = pl.BlockSpec(memory_space=pltpu.SMEM)
@@ -502,7 +548,7 @@
         buf(CLIPS * FULL, FULL, dtype=F32), buf(CLIPS * FULL, FULL),
         buf(HALF, FULL, dtype=F32), buf(HALF, FULL, dtype=F32), buf(HALF, FULL), buf(HALF, FULL),
         buf(HALF, HD, dtype=F32), buf(HALF, HD, dtype=F32),
-        pltpu.SemaphoreType.DMA((128,)), pltpu.SemaphoreType.DMA((128,)),
+        pltpu.SemaphoreType.DMA((192,)), pltpu.SemaphoreType.DMA((192,)),
         pltpu.SemaphoreType.DMA((8,)), pltpu.SemaphoreType.DMA((3,)), pltpu.SemaphoreType.DMA((3,)),
     ]
     student, tangent = pl.pallas_call(
@@ -514,6 +560,12 @@
         compiler_params=pltpu.CompilerParams(
             collective_id=0, has_side_effects=True, vmem_limit_bytes=60 * 2**20),
     )(clip_len, time_idx, x_t.reshape(rows, D), teacher_mod, student_mod, w_qkv, w_out)
+    student, tangent = pl.pallas_call(
+        hand_over,
+        out_shape=(out, out),
+        in_specs=[vmem, vmem],
+        out_specs=(vmem, vmem),
+    )(student, tangent)
     return (student.reshape(CLIPS, SEG, D), tangent.reshape(CLIPS, SEG, D))
 
 

time: 107 us -> 104 us (0.972)
  local copies, waits for them, and re-layouts: 3.53 us -> 0 us
    unnamed x2 -> x0, local copies, waits for them, and re-layouts: 3.53 us -> none
    pallas_call x0 -> x1, Pallas kernels: none -> 2.02 us  [on_device(): pl.pallas_call(hand_over, out_shape=(out, out), in_specs=[vmem, vmem], ou...]
    pallas_call x1, Pallas kernels: 102 us -> 101 us  [on_device(): pl.pallas_call(kernel, out_shape=(out, out), in_specs=[smem, smem, vmem,...]
where the time goes in v3:
time: 104 us
  Pallas kernels  103 us (99%)
    pallas_call x1, Pallas kernels, on_device(): pl.pallas_call(kernel, out_shape=(out, out), in_specs=[smem, smem, vmem,...  101 us

profile of v3, /device:TPU:1, one launch (start us, length us, event | category | flops | bytes accessed | tf_op | source)
XLA Modules:
  0.0 103.8 jit_solution(6922908740748954682)
XLA Ops:
  0.6 101.2 %shard_map.86 = (bf16[128,1536]{1,0:T(8,128)(2,1)}, bf16[128,1536]{1,0:T(8,128)(2,1)}) custom-call(s32[2]{0:T(128)} %len_ref.1, s32[2]{0:T(128)} %time_ref.1, bf16[128,1536]{1,0:T(8,128)(2,1)} %bitcast.3, f32[2,1536]{1,0:T(2,128)} %tmod_ref.1, f32[2,1536]{1,0:T(2,128)} %smod_ref.1, bf16[96,6144]{1,0:T(8,128)(2,1)} %wqkv_ref.1, bf16[128,1536]{1,0:T(8,128)(2,1)} %wout_ref.1), custom_call_target="tpu_custom_call" | custom-call | tf_op jit(solution)/shard_map/pallas_call | solution.py:554
  101.8 2.0 %shard_map.87 = (bf16[128,1536]{1,0:T(8,128)(2,1)}, bf16[128,1536]{1,0:T(8,128)(2,1)}) custom-call(bf16[128,1536]{1,0:T(8,128)(2,1)} %get-tuple-element.6.student_ref, bf16[128,1536]{1,0:T(8,128)(2,1)} %get-tuple-element.7.tangent_ref), custom_call_target="tpu_custom_call" | custom-call | tf_op jit(solution)/shard_map/pallas_call | solution.py:563

commit v4 on v3

--- a/solution.py
+++ b/solution.py
@@ -293,11 +293,26 @@
                     device_id=(member(slot, half), f), device_id_type=MESH,
                 ).start()
 
+    def send_students():
+        cols = pl.ds(mult(c * HD, HD), HD)
+        for half in range(2):
+            for slot in (7, 4, 5, 6, 3, 1, 2, 0):
+                src = mixed_s.at[:, pl.ds(half * HALF + slot * SEG, SEG)]
+                dst = attn_s.at[:, :, cols]
+                if half + slot == 0:
+                    pltpu.make_async_copy(src, dst, bulk_recv.at[1]).start()
+                else:
+                    pltpu.make_async_remote_copy(
+                        src_ref=src, dst_ref=dst, send_sem=bulk_send.at[1],
+                        recv_sem=bulk_recv.at[1],
+                        device_id=(member(slot, half), f), device_id_type=MESH,
+                    ).start()
+
     def all_received(phase, attn):
         pltpu.make_async_copy(attn, attn, bulk_recv.at[phase]).wait()
 
     def all_sent(phase, attn):
-        part = attn.at[:, pl.ds(0, INNER - HD)]
+        part = attn.at[..., pl.ds(0, INNER - HD)]
         pltpu.make_async_copy(part, part, bulk_send.at[phase]).wait()
 
     NT = (((1,), (1,)), ((), ()))
@@ -311,10 +326,11 @@
         key = jnp.concatenate([qkv[keys, HD:2 * HD], kmask[keys]], axis=1)
         out[...] = lax.dot_general(query, key, NT, preferred_element_type=F32)
 
-    def pipeline(first, second, third, between=lambda stage: None):
+    def pipeline(first, second, third, between=lambda stage: None, ready=lambda: None):
         first(0, 0)
         first(1, 1)
         second(0, 0)
+        ready()
         first(2, 0)
         second(1, 1)
         third(0, 0)
@@ -356,7 +372,7 @@
         probs = expo * (1.0 / jnp.sum(expo, axis=-1, keepdims=True))
         weights[rows] = probs.astype(BF16)
         scaled[rows] = probs * SCALE
-        mixed_s[rows] = jnp.dot(
+        mixed_s[blk // 2, pl.ds(blk % 2 * HALF, HALF)] = jnp.dot(
             weights[rows], qkv_s[keys, 2 * HD:], preferred_element_type=F32).astype(BF16)
 
     def tangent_scores(blk, p):
@@ -383,7 +399,7 @@
         def tile(n, _):
             cols = pl.ds(mult(n * 512, 512), 512)
             out[:, cols] = jnp.dot(
-                attn[...], wo[:, cols], preferred_element_type=F32).astype(BF16)
+                attn[...].reshape(CLIPS * SEG, INNER), wo[:, cols], preferred_element_type=F32).astype(BF16)
             return 0
 
         lax.fori_loop(0, 3, tile, 0)
@@ -500,17 +516,21 @@
     gd.step5()
     project(dg, 0, qkv_d, other_d)
     project(dg, HALF, qkv_d, other_d)
-    swaps_d = [exchange(clip, 0, qkv_d, other_d) for clip in range(2)]
+    swaps_0 = [exchange(0, 0, qkv_d, other_d)]
+    swaps_1 = [exchange(1, 0, qkv_d, other_d)]
     gd.end_a()
     project(dg, BLK, qkv_d, other_d)
-    swaps_d.append(exchange(0, 1, qkv_d, other_d))
-    gd.end_b()
-    project(dg, HALF + BLK, qkv_d, other_d)
-    swaps_d.append(exchange(1, 1, qkv_d, other_d))
-    for blk in range(4):
-        send_block(blk, 1, mixed_s, attn_s)
-    arrived(*swaps_d)
-    pipeline(tangent_scores, tangent_probs, tangent_values)
+    swaps_0.append(exchange(0, 1, qkv_d, other_d))
+
+    def second_clip():
+        gd.end_b()
+        project(dg, HALF + BLK, qkv_d, other_d)
+        swaps_1.append(exchange(1, 1, qkv_d, other_d))
+        send_students()
+        arrived(*swaps_1)
+
+    arrived(*swaps_0)
+    pipeline(tangent_scores, tangent_probs, tangent_values, ready=second_clip)
     all_received(1, attn_s)
     output(attn_s, student_ref)
     all_received(2, attn_d)
@@ -542,8 +562,8 @@
         buf(CLIPS * FULL, 384), buf(CLIPS * FULL, 384), buf(CLIPS * FULL, 384),
         buf(CLIPS * HALF, 384), buf(CLIPS * HALF, 384), buf(CLIPS * HALF, 384),
         buf(CLIPS * HALF, D), buf(CLIPS * HALF, D), buf(8, D, dtype=F32), buf(CLIPS * FULL, HD),
-        buf(CLIPS * FULL, HD), buf(CLIPS * FULL, HD), buf(CLIPS * FULL, HD),
-        buf(rows, INNER), buf(rows, INNER), buf(rows, INNER),
+        buf(CLIPS * FULL, HD), buf(CLIPS, FULL, HD), buf(CLIPS * FULL, HD),
+        buf(rows, INNER), buf(CLIPS, SEG, INNER), buf(rows, INNER),
         buf(rows, D), buf(rows, D),
         buf(CLIPS * FULL, FULL, dtype=F32), buf(CLIPS * FULL, FULL),
         buf(HALF, FULL, dtype=F32), buf(HALF, FULL, dtype=F32), buf(HALF, FULL), buf(HALF, FULL),

time: 104 us -> 106 us (1.019)
  Pallas kernels: 103 us -> 105 us
    pallas_call x1, Pallas kernels: 101 us -> 103 us  [on_device(): pl.pallas_call(kernel, out_shape=(out, out), in_specs=[smem, smem, vmem,...]
where the time goes in v4:
time: 106 us
  Pallas kernels  105 us (99%)
    pallas_call x1, Pallas kernels, on_device(): pl.pallas_call(kernel, out_shape=(out, out), in_specs=[smem, smem, vmem,...  103 us

profile of v4, /device:TPU:1, one launch (start us, length us, event | category | flops | bytes accessed | tf_op | source)
XLA Modules:
  0.0 105.7 jit_solution(1853617164820588613)
XLA Ops:
  0.6 103.0 %shard_map.86 = (bf16[128,1536]{1,0:T(8,128)(2,1)}, bf16[128,1536]{1,0:T(8,128)(2,1)}) custom-call(s32[2]{0:T(128)} %len_ref.1, s32[2]{0:T(128)} %time_ref.1, bf16[128,1536]{1,0:T(8,128)(2,1)} %bitcast.3, f32[2,1536]{1,0:T(2,128)} %tmod_ref.1, f32[2,1536]{1,0:T(2,128)} %smod_ref.1, bf16[96,6144]{1,0:T(8,128)(2,1)} %wqkv_ref.1, bf16[128,1536]{1,0:T(8,128)(2,1)} %wout_ref.1), custom_call_target="tpu_custom_call" | custom-call | tf_op jit(solution)/shard_map/pallas_call | solution.py:574
  103.7 2.0 %shard_map.87 = (bf16[128,1536]{1,0:T(8,128)(2,1)}, bf16[128,1536]{1,0:T(8,128)(2,1)}) custom-call(bf16[128,1536]{1,0:T(8,128)(2,1)} %get-tuple-element.6.student_ref, bf16[128,1536]{1,0:T(8,128)(2,1)} %get-tuple-element.7.tangent_ref), custom_call_target="tpu_custom_call" | custom-call | tf_op jit(solution)/shard_map/pallas_call | solution.py:583

commit v5 on v4

--- a/solution.py
+++ b/solution.py
@@ -25,7 +25,7 @@
 F32 = jnp.float32
 BF16 = jnp.bfloat16
 
-RING = 256
+RING = 384
 
 S00, S01, S03, S10, S02, S11, S13, S12 = range(8)
 
@@ -326,11 +326,10 @@
         key = jnp.concatenate([qkv[keys, HD:2 * HD], kmask[keys]], axis=1)
         out[...] = lax.dot_general(query, key, NT, preferred_element_type=F32)
 
-    def pipeline(first, second, third, between=lambda stage: None, ready=lambda: None):
+    def pipeline(first, second, third, between=lambda stage: None):
         first(0, 0)
         first(1, 1)
         second(0, 0)
-        ready()
         first(2, 0)
         second(1, 1)
         third(0, 0)
@@ -516,21 +515,16 @@
     gd.step5()
     project(dg, 0, qkv_d, other_d)
     project(dg, HALF, qkv_d, other_d)
-    swaps_0 = [exchange(0, 0, qkv_d, other_d)]
-    swaps_1 = [exchange(1, 0, qkv_d, other_d)]
+    swaps_d = [exchange(clip, 0, qkv_d, other_d) for clip in range(2)]
     gd.end_a()
     project(dg, BLK, qkv_d, other_d)
-    swaps_0.append(exchange(0, 1, qkv_d, other_d))
-
-    def second_clip():
-        gd.end_b()
-        project(dg, HALF + BLK, qkv_d, other_d)
-        swaps_1.append(exchange(1, 1, qkv_d, other_d))
-        send_students()
-        arrived(*swaps_1)
-
-    arrived(*swaps_0)
-    pipeline(tangent_scores, tangent_probs, tangent_values, ready=second_clip)
+    swaps_d.append(exchange(0, 1, qkv_d, other_d))
+    gd.end_b()
+    project(dg, HALF + BLK, qkv_d, other_d)
+    swaps_d.append(exchange(1, 1, qkv_d, other_d))
+    send_students()
+    arrived(*swaps_d)
+    pipeline(tangent_scores, tangent_probs, tangent_values)
     all_received(1, attn_s)
     output(attn_s, student_ref)
     all_received(2, attn_d)

time: 106 us -> 103 us (0.972)
  Pallas kernels: 105 us -> 103 us
    pallas_call x1, Pallas kernels: 103 us -> 101 us  [on_device(): pl.pallas_call(kernel, out_shape=(out, out), in_specs=[smem, smem, vmem,...]
where the time goes in v5:
time: 103 us
  Pallas kernels  103 us (100%)
    pallas_call x1, Pallas kernels, on_device(): pl.pallas_call(kernel, out_shape=(out, out), in_specs=[smem, smem, vmem,...  101 us

profile of v5, /device:TPU:1, one launch (start us, length us, event | category | flops | bytes accessed | tf_op | source)
XLA Modules:
  0.0 103.2 jit_solution(14340876933500089886)
XLA Ops:
  0.6 100.6 %shard_map.86 = (bf16[128,1536]{1,0:T(8,128)(2,1)}, bf16[128,1536]{1,0:T(8,128)(2,1)}) custom-call(s32[2]{0:T(128)} %len_ref.1, s32[2]{0:T(128)} %time_ref.1, bf16[128,1536]{1,0:T(8,128)(2,1)} %bitcast.3, f32[2,1536]{1,0:T(2,128)} %tmod_ref.1, f32[2,1536]{1,0:T(2,128)} %smod_ref.1, bf16[96,6144]{1,0:T(8,128)(2,1)} %wqkv_ref.1, bf16[128,1536]{1,0:T(8,128)(2,1)} %wout_ref.1), custom_call_target="tpu_custom_call" | custom-call | tf_op jit(solution)/shard_map/pallas_call | solution.py:568
  101.2 2.0 %shard_map.87 = (bf16[128,1536]{1,0:T(8,128)(2,1)}, bf16[128,1536]{1,0:T(8,128)(2,1)}) custom-call(bf16[128,1536]{1,0:T(8,128)(2,1)} %get-tuple-element.6.student_ref, bf16[128,1536]{1,0:T(8,128)(2,1)} %get-tuple-element.7.tangent_ref), custom_call_target="tpu_custom_call" | custom-call | tf_op jit(solution)/shard_map/pallas_call | solution.py:577
